TPU v7x, 32 devices: a whole 2x2x4 slice. The times are simulated.
32 devices in a mesh: groups: 1, solve: 32 (over z, y, x, core).
Axes of the slice: x: 2, y: 2, z: 4, core: 2. Of those that a mesh axis runs over, the one named last changes fastest.
Arguments:
- beliefs: bfloat16 [16384, 2652], P(('groups', 'solve')), may hold values from 0.099609375 to 2
- targets: bfloat16 [16384, 2652], P(('groups', 'solve')), may hold values from -3 to 3
- leaf_line: int32 [16384], P(('groups', 'solve')), may hold values from 0 to 31
- turn_card: int32 [16384], P(('groups', 'solve')), may hold values from 0 to 51
- encoder: bfloat16 [2652, 1024], P(None, 'solve'), may hold values from -0.125 to 0.125
- value_head: bfloat16 [1024, 2652], P('solve'), may hold values from -0.1875 to 0.1875
- regrets: float32 [32, 1326], P(('groups', 'solve')), may hold values from -1.5 to 1.5
Outputs:
- new_regrets: float32 [32, 1326], P(('groups', 'solve'))
- line_values: float32 [32, 2652], P(('groups', 'solve'))
- head_grad: float32 [1024, 2652], P(('groups', 'solve'))
All inputs are finite; a program needn't handle non-finite values.
Results may differ from a plain program's by a relative error of at most 0.004.
Values may be sent and summed in bfloat16 or wider, within the bound.
A program may use at most 128 MiB of HBM per device.

v0:
```python
import jax
import jax.numpy as jnp
import numpy as np
from jax import lax
from jax.sharding import PartitionSpec as P

open_turns = 45.0
regret_floor = 0.05


def blocker_table(hand_count):
    blockers = np.zeros((52, hand_count), np.float32)
    column = 0
    for low_card in range(52):
        for high_card in range(low_card + 1, 52):
            blockers[low_card, column] = 1.0
            blockers[high_card, column] = 1.0
            column = column + 1
    return blockers


def per_device(beliefs, targets, leaf_line, turn_card, encoder, value_head, regrets):
    devices = lax.axis_size("solve")
    leaf_count = beliefs.shape[0]
    hand_count = regrets.shape[1]
    local_lines = regrets.shape[0]
    line_count = local_lines * devices
    hidden = jax.nn.silu(
        jnp.dot(
            beliefs,
            lax.all_gather(encoder, "solve", axis=1, tiled=True),
            preferred_element_type=jnp.float32,
        )
    ).astype(jnp.bfloat16)
    output = jnp.dot(
        hidden,
        lax.all_gather(value_head, "solve", axis=0, tiled=True),
        preferred_element_type=jnp.float32,
    )
    errors = ((output - targets.astype(jnp.float32)) / leaf_count).astype(jnp.bfloat16)
    head_grad = lax.psum_scatter(
        lax.dot_general(
            hidden, errors, (((0,), (0,)), ((), ())), preferred_element_type=jnp.float32
        ),
        "solve",
        scatter_dimension=0,
        tiled=True,
    )
    leaf_value = output.astype(jnp.bfloat16).astype(jnp.float32)
    blockers = jnp.asarray(blocker_table(hand_count), dtype=jnp.float32)
    card_onehot = (turn_card[:, None] == jnp.arange(52, dtype=jnp.int32)[None, :]).astype(
        jnp.float32
    )
    blocked = jnp.dot(
        card_onehot, blockers, precision=lax.Precision.HIGHEST, preferred_element_type=jnp.float32
    )
    open_share = (1.0 - blocked) / open_turns
    weighted = leaf_value * jnp.concatenate([open_share, open_share], 1)
    line_onehot = (leaf_line[:, None] == jnp.arange(line_count, dtype=jnp.int32)[None, :]).astype(
        jnp.float32
    )
    line_values = lax.psum_scatter(
        lax.dot_general(
            line_onehot,
            weighted,
            (((0,), (0,)), ((), ())),
            precision=lax.Precision.HIGHEST,
            preferred_element_type=jnp.float32,
        ),
        "solve",
        scatter_dimension=0,
        tiled=True,
    )
    positive = jnp.maximum(regrets, 0.0) + regret_floor
    denominator, numerator = lax.psum(
        (jnp.sum(positive, 0), jnp.sum(positive * line_values[:, :hand_count], 0)), "solve"
    )
    root_value = numerator / denominator
    new_regrets = regrets + line_values[:, :hand_count] - root_value[None, :]
    return (new_regrets, line_values, head_grad)


def solution(mesh):
    placed = (
        P(("groups", "solve"), None),
        P(("groups", "solve"), None),
        P(("groups", "solve")),
        P(("groups", "solve")),
        P(None, "solve"),
        P("solve", None),
        P(("groups", "solve"), None),
    )
    return jax.shard_map(
        per_device,
        mesh=mesh,
        in_specs=placed,
        out_specs=(
            P(("groups", "solve"), None),
            P(("groups", "solve"), None),
            P(("groups", "solve"), None),
        ),
        check_vma=False,
    )
```

profile of v0, /device:TPU:0, one launch (start us, length us, event | category | flops | bytes accessed | tf_op | source)
XLA Modules:
  0.0 443.6 jit_solution(16921951140862786265)
XLA Ops:
  7.2 0.0 copy-start
  7.2 0.0 all-gather.3.cloned.1.call-start
  7.2 0.7 all-gather.3.cloned.1.call-update
  7.9 0.0 all-gather.5.cloned.1.call-start
  8.0 0.7 all-gather.5.cloned.1.call-update
  8.7 0.0 all-reduce.4.cloned.1.call-start
  8.7 3.9 fusion.4
  12.6 67.1 %all-gather.3.cloned.1.call-done = bf16[2652,1024]{0,1:T(8,128)(2,1)} async-done(((bf16[2652,32]{0,1:T(8,128)(2,1)}), bf16[2652,1024]{0,1:T(8,128)(2,1)}) %all-gather.3.cloned.1.call-update) | async-done | bytes 5431312 | tf_op jit(solution)/shard_map/all_gather | solution.py:31
  79.7 0.0 copy-done
  79.7 7.1 %fusion.16 = f32[512,1024]{1,0:T(8,128)} fusion(bf16[512,2652]{0,1:T(8,128)(2,1)S(1)} %copy-done, bf16[2652,1024]{0,1:T(8,128)(2,1)} %all-gather.3.cloned.1.call-done), kind=kOutput, calls=%fused_computation.25 | convolution fusion | flops 2780823552 | bytes 10244096 | tf_op jit(solution)/shard_map/dot_general | solution.py:29
  86.8 0.0 copy-start.4
  86.8 60.9 %all-gather.5.cloned.1.call-done = bf16[1024,2652]{1,0:T(8,128)(2,1)} async-done(((bf16[32,2652]{1,0:T(8,128)(2,1)}), bf16[1024,2652]{1,0:T(8,128)(2,1)}) %all-gather.5.cloned.1.call-update) | async-done | bytes 5431312 | tf_op jit(solution)/shard_map/all_gather | solution.py:37
  147.7 0.0 copy-start.1
  147.7 6.2 %fusion.15 = f32[512,2652]{0,1:T(8,128)S(1)} fusion(bf16[1024,2652]{1,0:T(8,128)(2,1)} %all-gather.5.cloned.1.call-done, f32[512,1024]{1,0:T(8,128)} %fusion.16), kind=kOutput, calls=%fused_computation.24 | convolution fusion | flops 2783444992 | bytes 12959744 | tf_op jit(solution)/shard_map/dot_general | solution.py:35
  154.0 0.0 copy-start.2
  154.0 2.3 copy-done.2
  156.3 0.0 copy-done.4
  156.3 0.0 copy-done.1
  156.3 3.9 fusion
  160.2 0.0 all-reduce.4.cloned.1.call-update
  160.2 0.2 reduce-scatter.2.cloned.1.call-start
  160.4 11.7 %fusion.5 = f32[1024,2652]{1,0:T(8,128)} fusion(f32[512,2652]{0,1:T(8,128)} %copy-done.2, bf16[512,2652]{0,1:T(8,128)(2,1)} %param.9, f32[512,1024]{1,0:T(8,128)} %fusion.16), kind=kOutput, calls=%fused_computation.8 | convolution fusion | flops 2788876288 | bytes 21106688 | tf_op jit(solution)/shard_map/dot_general | solution.py:42
  172.1 0.0 copy-start.3
  172.1 0.0 reduce-scatter.2.cloned.1.call-update
  172.2 112.9 %all-reduce.4.cloned.1.call-done = f32[32,2652]{1,0:T(8,128)} async-done(((f32[32,2652]{1,0:T(8,128)}), f32[32,2652]{1,0:T(8,128)}) %all-reduce.4.cloned.1.call-update) | async-done | bytes 339472
  285.1 0.0 copy-done.3
  285.1 0.8 fusion.12
  285.9 41.3 %all-reduce.1 = (f32[1326]{0:T(1024)S(1)}, f32[1326]{0:T(1024)S(1)}) all-reduce(f32[1326]{0:T(1024)S(1)} %get-tuple-element.4, f32[1326]{0:T(1024)S(1)} %get-tuple-element.3), channel_id=1, replica_groups=mesh['groups'=1,'solve'=32] {'solve'}, use_global_device_ids=true, to_apply=%region_1.2 | all-reduce | flops 2652 | bytes 21216 | tf_op jit(solution)/shard_map/psum | solution.py:75
  327.2 1.5 constant_dynamic-slice_fusion
  328.7 1.4 reshape_subtract_fusion
  330.1 107.0 %reduce-scatter.2.cloned.1.call-done = f32[32,2652]{1,0:T(8,128)} async-done(((f32[1024,2652]{1,0:T(8,128)}), f32[32,2652]{1,0:T(8,128)}) %reduce-scatter.2.cloned.1.call-update) | async-done | bytes 339472 | tf_op jit(solution)/shard_map/reduce_scatter | solution.py:41
  (1 shorter events, 0.0 us)
Async XLA Ops:
  7.2 72.6 %copy-start = (bf16[512,2652]{0,1:T(8,128)(2,1)S(1)}, bf16[512,2652]{0,1:T(8,128)(2,1)}, u32[]{:S(2)}) copy-start(bf16[512,2652]{0,1:T(8,128)(2,1)} %param.8) | copy-start | bytes 8146948
  7.2 72.6 %all-gather.3.cloned.1.call-start = ((), (), s32[]{:S(2)}) async-start(), calls=%async_computation.1 | async-start | bytes 5677056 | tf_op jit(solution)/shard_map/all_gather | solution.py:31
  7.9 139.8 %all-gather.5.cloned.1.call-start = ((), (), s32[]{:S(2)}) async-start(), calls=%async_computation.2 | async-start | bytes 5677056 | tf_op jit(solution)/shard_map/all_gather | solution.py:37
  8.7 276.4 %all-reduce.4.cloned.1.call-start = ((), (), s32[]{:S(2)}) async-start(), calls=%async_computation.4 | async-start | bytes 688128
  86.8 69.5 %copy-start.4 = (s32[512]{0:T(512)S(1)}, s32[512]{0:T(512)}, u32[]{:S(2)}) copy-start(s32[512]{0:T(512)} %param.10) | copy-start | bytes 6148
  147.7 8.6 %copy-start.1 = (f32[512,1326]{0,1:T(8,128)S(1)}, f32[512,1326]{0,1:T(8,128)}, u32[]{:S(2)}) copy-start(f32[512,1326]{0,1:T(8,128)} %fusion.4) | copy-start | bytes 8146948
  154.0 2.3 copy-start.2
  160.2 276.9 %reduce-scatter.2.cloned.1.call-start = ((), (), s32[]{:S(2)}) async-start(), calls=%async_computation.3 | async-start | bytes 11354112 | tf_op jit(solution)/shard_map/reduce_scatter | solution.py:41
  172.1 113.0 %copy-start.3 = (f32[1,1326]{1,0:T(1,128)S(1)}, f32[1,1326]{1,0:T(1,128)}, u32[]{:S(2)}) copy-start(f32[1,1326]{1,0:T(1,128)} %param.14) | copy-start | bytes 15916
Sparse Core Ops, SparseCore 0:
  10.9 68.7 all-gather.2
  82.6 65.0 all-gather.4
  160.3 124.7 all-reduce.3
  292.5 144.5 reduce-scatter.1
where the time goes:
time: 444 us
  waiting for transfers between devices  349 us (79%)
  blocking collectives  41.3 us (9%)
  matrix products  32.8 us (7%)
  between operations  13.8 us (3%)
    unnamed x5, waiting for transfers between devices  114 us
    reduce_scatter x1, waiting for transfers between devices, per_device(): lax.psum_scatter(lax.dot_general(hidden, errors, (((0,), (0,)), ((), ()))...  107 us
    all_gather x1, waiting for transfers between devices, per_device(): lax.all_gather(encoder, 'solve', axis=1, tiled=True)  67.1 us
    all_gather x1, waiting for transfers between devices, per_device(): lax.all_gather(value_head, 'solve', axis=0, tiled=True)  60.9 us
    psum x1, blocking collectives, per_device(): lax.psum((jnp.sum(positive, 0), jnp.sum(positive * line_values[:, :hand_c...  41.3 us
    dot_general x1, matrix products, per_device(): lax.dot_general(hidden, errors, (((0,), (0,)), ((), ())), preferred_eleme...  11.7 us
  transfers between devices with their start and end apart: 4, of which 4 were waited for; matrix products, arithmetic and copies ran while one was open for 6% of the time, Pallas kernels for 0%

commit v1 on v0

v1 whole, which is shorter than its diff:
```python
import functools

import jax
import jax.numpy as jnp
import numpy as np
from jax import lax
from jax.experimental import pallas as pl
from jax.experimental.pallas import tpu as pltpu
from jax.sharding import PartitionSpec as P

open_turns = 45.0
regret_floor = 0.05
MESH = pl.DeviceIdType.MESH
F32, BF16 = jnp.float32, jnp.bfloat16
NUM_AT, MSG = 2688, 4096


def blocker_table(hand_count, rows=52):
    blockers = np.zeros((rows, hand_count), np.float32)
    column = 0
    for low_card in range(52):
        for high_card in range(low_card + 1, 52):
            blockers[low_card, column] = 1.0
            blockers[high_card, column] = 1.0
            column = column + 1
    return blockers


def step_kernel(
    nz, hands,
    beliefs, targets, line, card, enc, head, regrets, blockers,
    new_regrets, line_values, head_grad,
    w1, w2, opened, leaf, errors, hidden, hidden_t, partial,
    sib_send, sib_recv, diag_send, diag_recv, xy_send, xy_recv, z_send, z_recv,
    lines_part, msg, msg_in, all_regrets,
    ag_s, ag_r, rs_s, rs_r, reg_s, reg_r, msg_s, msg_r,
):
    n = nz * 8
    rows = enc.shape[0]
    half = rows // 2
    plane = rows * 8
    leaves, width = beliefs.shape
    me = lax.axis_index("solve")
    c = lax.rem(me, 2)
    x = lax.rem(me // 2, 2)
    y = lax.rem(me // 4, 2)
    z = me // 8

    def dev(zz, yy, xx, cc):
        return zz * 8 + yy * 4 + xx * 2 + cc

    def zat(dz):
        return lax.rem(z + dz, nz)

    sib, xn, yn = dev(z, y, x, 1 - c), dev(z, y, 1 - x, c), dev(z, 1 - y, x, c)

    def block(d, start=0, count=rows):
        return pl.ds(pl.multiple_of(d * rows + start, 16), count)

    def remote(src, dst, ss, rs, to):
        return pltpu.make_async_remote_copy(
            src_ref=src, dst_ref=dst, send_sem=ss, recv_sem=rs,
            device_id={"solve": to}, device_id_type=MESH,
        )

    barrier = pltpu.get_barrier_semaphore()

    def greet(i, _):
        pl.semaphore_signal(
            barrier, inc=1, device_id={"solve": lax.rem(me + i, n)}, device_id_type=MESH
        )
        return _

    lax.fori_loop(1, n, greet, 0)
    pl.semaphore_wait(barrier, n - 1)

    started = []
    used = [0, 0]

    def gather_send(k, src_dev, to, part=None, own=None):
        w = (w1, w2)[k]
        span = (0, rows) if part is None else (part * half, half)
        place = w.at[block(src_dev, *span)]
        slot = used[k]
        used[k] += 1
        rsem = ag_r.at[k, src_dev] if part != 1 else ag_r.at[k, n + src_dev // 8]
        cp = remote(place if own is None else own, place, ag_s.at[k, slot], rsem, to)
        cp.start()
        started.append(cp)

    def gather_wait(k, src_dev, part=None):
        w = (w1, w2)[k]
        span = (0, rows) if part is None else (part * half, half)
        place = w.at[block(src_dev, *span)]
        rsem = ag_r.at[k, src_dev] if part != 1 else ag_r.at[k, n + src_dev // 8]
        remote(place, place, ag_s.at[k, 0], rsem, sib).wait_recv()

    for k, own in ((0, enc), (1, head)):
        for dz in (1, nz - 1, 2):
            gather_send(k, me, dev(zat(dz), y, x, c), own=own)
        for to in (xn, yn, sib):
            gather_send(k, me, to, own=own)

    all_regrets[me] = regrets[...]

    def send_regrets(i, _):
        remote(
            all_regrets.at[me], all_regrets.at[me], reg_s, reg_r, lax.rem(me + i, n)
        ).start()
        return _

    lax.fori_loop(1, n, send_regrets, 0)
    w1[block(me)] = enc[...]
    w2[block(me)] = head[...]

    def forward_column(k, dz):
        src = dev(zat(dz), y, x, c)
        gather_wait(k, src)
        for to in (xn, yn, sib):
            gather_send(k, src, to)

    def forward_plane(k, dz):
        src = dev(zat(dz), y, 1 - x, c)
        gather_wait(k, src)
        gather_send(k, src, yn, part=0)
        gather_send(k, src, sib)
        src = dev(zat(dz), 1 - y, x, c)
        gather_wait(k, src)
        gather_send(k, src, xn, part=1)
        gather_send(k, src, sib)

    def forward_diagonal(k, dz):
        src = dev(zat(dz), 1 - y, 1 - x, c)
        gather_wait(k, src, 0)
        gather_wait(k, src, 1)
        gather_send(k, src, sib)

    def wait_sibling(k, dz):
        for yy in (0, 1):
            for xx in (0, 1):
                gather_wait(k, dev(zat(dz), yy, xx, 1 - c))

    for k in (0, 1):
        for dz in (1, nz - 1, 2):
            forward_column(k, dz)
    card_onehot = (
        lax.broadcasted_iota(jnp.int32, (leaves, blockers.shape[0]), 1) == card[...]
    ).astype(F32).astype(BF16)
    for start in range(0, width, 256):
        cols = slice(start, min(start + 256, width))
        opened[:, cols] = (
            1.0 - jnp.dot(card_onehot, blockers[:, cols], preferred_element_type=F32)
        ).astype(BF16)
    for dz in (0, 1, nz - 1, 2):
        forward_plane(0, dz)
    for dz in (0, 1, nz - 1, 2):
        forward_plane(1, dz)
    for dz in (0, 1, nz - 1, 2):
        forward_diagonal(0, dz)

    for dz in (0, 1, nz - 1, 2):
        wait_sibling(0, dz)
        units = pl.ds(pl.multiple_of(zat(dz) * plane, plane), plane)
        pre = lax.dot_general(
            beliefs[...], w1[units, :], (((1,), (1,)), ((), ())), preferred_element_type=F32
        )
        act = pre / (1.0 + jnp.exp(-pre))
        hidden[:, units] = act.astype(BF16)
        hidden_t[units, :] = act.T.astype(BF16)
        forward_diagonal(1, dz)
    for dz in (0, 1, nz - 1, 2):
        wait_sibling(1, dz)

    def output_columns(cols):
        out = jnp.dot(hidden[...], w2[:, cols], preferred_element_type=F32)
        errors[:, cols] = ((out - targets[:, cols].astype(F32)) * (1.0 / leaves)).astype(BF16)
        leaf[:, cols] = out.astype(BF16)

    full = width // 256

    def output_step(j, _):
        output_columns(pl.ds(pl.multiple_of(j * 256, 256), 256))
        return _

    lax.fori_loop(0, full, output_step, 0)
    if full * 256 < width:
        output_columns(slice(full * 256, width))

    order = (1, nz - 1, 2, 0)
    pend = {}
    rs_used = [0]

    def reduce_send(name, src, dst, to):
        slot = rs_used[0]
        rs_used[0] += 1
        cp = remote(src, dst, rs_s.at[slot], rs_r.at[slot], to)
        cp.start()
        started.append(cp)
        pend[name] = cp

    def in_plane(yy, xx, cc):
        return pl.ds(pl.multiple_of((yy * 4 + xx * 2 + cc) * rows, rows), rows)

    rel = ((y, x), (y, 1 - x), (1 - y, x), (1 - y, 1 - x))

    def compute(p):
        units = pl.ds(pl.multiple_of(zat(order[p]) * plane, plane), plane)
        partial[p] = jnp.dot(hidden_t[units, :], errors[...], preferred_element_type=F32)
        for r in (3, 1, 2, 0):
            yy, xx = rel[r]
            sib_send[p, r] = partial[p, in_plane(yy, xx, 1 - c)].astype(BF16)
            reduce_send(("s", p, r), sib_send.at[p, r], sib_recv.at[p, r], sib)

    def chip_sum(p, r, lo=0, count=rows):
        yy, xx = rel[r]
        base = (yy * 4 + xx * 2 + c) * rows + lo
        own = partial[p, pl.ds(pl.multiple_of(base, 16), count)]
        return own + sib_recv[p, r, lo:lo + count].astype(F32)

    def stage_diagonal(p):
        pend["s", p, 3].wait_recv()
        diag_send[p] = chip_sum(p, 3).astype(BF16)
        reduce_send(("a", p), diag_send.at[p, pl.ds(0, half)], diag_recv.at[p, pl.ds(0, half)], yn)
        reduce_send(("b", p), diag_send.at[p, pl.ds(half, half)], diag_recv.at[p, pl.ds(half, half)], xn)

    def stage_neighbours(p):
        pend["s", p, 1].wait_recv()
        pend["a", p].wait_recv()
        xy_send[p, 0, :half] = (chip_sum(p, 1, 0, half) + diag_recv[p, :half].astype(F32)).astype(BF16)
        xy_send[p, 0, half:] = chip_sum(p, 1, half, half).astype(BF16)
        reduce_send(("x", p), xy_send.at[p, 0], xy_recv.at[p, 0], xn)
        pend["s", p, 2].wait_recv()
        pend["b", p].wait_recv()
        xy_send[p, 1, :half] = chip_sum(p, 2, 0, half).astype(BF16)
        xy_send[p, 1, half:] = (chip_sum(p, 2, half, half) + diag_recv[p, half:].astype(F32)).astype(BF16)
        reduce_send(("y", p), xy_send.at[p, 1], xy_recv.at[p, 1], yn)

    def column_sum(p):
        pend["s", p, 0].wait_recv()
        pend["x", p].wait_recv()
        pend["y", p].wait_recv()
        return chip_sum(p, 0) + xy_recv[p, 0].astype(F32) + xy_recv[p, 1].astype(F32)

    def stage_column(p):
        z_send[p] = column_sum(p).astype(BF16)
        reduce_send(("z", p), z_send.at[p], z_recv.at[p], dev(zat(order[p]), y, x, c))

    def line_messages():
        remote(all_regrets.at[pl.ds(0, n - 1)], all_regrets.at[pl.ds(0, n - 1)], reg_s, reg_r, sib).wait_recv()
        onehot = (
            lax.broadcasted_iota(jnp.int32, (n, leaves), 0) == line[...]
        ).astype(F32).astype(BF16)
        for start in range(0, width, 512):
            cols = slice(start, min(start + 512, width))
            masked = (leaf[:, cols].astype(F32) * opened[:, cols].astype(F32)).astype(BF16)
            lines_part[:, cols] = jnp.dot(onehot, masked, preferred_element_type=F32) / open_turns
        numer = jnp.zeros((1, hands), F32)
        for l in range(n):
            row = lines_part[l:l + 1, :]
            msg[l, :, 0:width] = row
            numer += (jnp.maximum(all_regrets[l], 0.0) + regret_floor) * row[:, :hands]
        for l in range(n):
            msg[l, :, NUM_AT:NUM_AT + hands] = numer
        msg_in[me] = msg[me]

        def send(i, _):
            to = lax.rem(me + i, n)
            remote(msg.at[to], msg_in.at[me], msg_s, msg_r, to).start()
            return _

        lax.fori_loop(1, n, send, 0)

    compute(0)
    compute(1)
    stage_diagonal(0)
    compute(2)
    stage_diagonal(1)
    stage_neighbours(0)
    compute(3)
    stage_diagonal(2)
    stage_neighbours(1)
    stage_diagonal(3)
    stage_column(0)
    line_messages()
    stage_neighbours(2)
    stage_column(1)
    stage_neighbours(3)
    stage_column(2)

    remote(msg_in.at[pl.ds(0, n - 1)], msg_in.at[pl.ds(0, n - 1)], msg_s, msg_r, sib).wait_recv()
    total = jnp.zeros((1, MSG), F32)
    denominator = jnp.zeros((1, hands), F32)
    for l in range(n):
        total += msg_in[l]
        denominator += jnp.maximum(all_regrets[l], 0.0) + regret_floor
    line_values[...] = total[:, :width]
    root = total[:, NUM_AT:NUM_AT + hands] / denominator
    new_regrets[...] = regrets[...] + total[:, :hands] - root

    result = column_sum(3)
    for p in range(3):
        pend["z", p].wait_recv()
        result += z_recv[p].astype(F32)
    head_grad[...] = result

    for cp in started:
        cp.wait_send()
    remote(all_regrets.at[pl.ds(0, n - 1)], all_regrets.at[pl.ds(0, n - 1)], reg_s, reg_r, sib).wait_send()
    remote(msg.at[pl.ds(0, n - 1)], msg.at[pl.ds(0, n - 1)], msg_s, msg_r, sib).wait_send()


def fused(nz, beliefs, targets, leaf_line, turn_card, encoder, value_head, regrets):
    n = nz * 8
    leaves, width = beliefs.shape
    hands = regrets.shape[1]
    rows = value_head.shape[0]
    units = rows * n
    table = blocker_table(hands, 64)
    blockers = jnp.asarray(np.concatenate([table, table], 1), dtype=BF16)
    vm = pl.BlockSpec(memory_space=pltpu.VMEM)
    dma = pltpu.SemaphoreType.DMA
    return pl.pallas_call(
        functools.partial(step_kernel, nz, hands),
        out_shape=(
            jax.ShapeDtypeStruct((1, hands), F32),
            jax.ShapeDtypeStruct((1, width), F32),
            jax.ShapeDtypeStruct((rows, width), F32),
        ),
        in_specs=[vm] * 8,
        out_specs=(vm, vm, vm),
        scratch_shapes=[
            pltpu.VMEM((units, width), BF16),
            pltpu.VMEM((units, width), BF16),
            pltpu.VMEM((leaves, width), BF16),
            pltpu.VMEM((leaves, width), BF16),
            pltpu.VMEM((leaves, width), BF16),
            pltpu.VMEM((leaves, units), BF16),
            pltpu.VMEM((units, leaves), BF16),
            pltpu.VMEM((4, rows * 8, width), F32),
            pltpu.VMEM((4, 4, rows, width), BF16),
            pltpu.VMEM((4, 4, rows, width), BF16),
            pltpu.VMEM((4, rows, width), BF16),
            pltpu.VMEM((4, rows, width), BF16),
            pltpu.VMEM((4, 2, rows, width), BF16),
            pltpu.VMEM((4, 2, rows, width), BF16),
            pltpu.VMEM((3, rows, width), BF16),
            pltpu.VMEM((3, rows, width), BF16),
            pltpu.VMEM((n, width), F32),
            pltpu.VMEM((n, 1, MSG), F32),
            pltpu.VMEM((n, 1, MSG), F32),
            pltpu.VMEM((n, 1, hands), F32),
            dma((2, 40)),
            dma((2, n + nz)),
            dma((40,)),
            dma((40,)),
            dma, dma, dma, dma,
        ],
        compiler_params=pltpu.CompilerParams(
            collective_id=0, has_side_effects=True, vmem_limit_bytes=60 * 2**20
        ),
        cost_estimate=pl.CostEstimate(
            flops=6 * leaves * width * units, bytes_accessed=12 * 2**20, transcendentals=leaves * units
        ),
    )(
        beliefs, targets, leaf_line.reshape(1, leaves), turn_card.reshape(leaves, 1),
        encoder.T, value_head, regrets, blockers,
    )


def by_collectives(beliefs, targets, leaf_line, turn_card, encoder, value_head, regrets):
    devices = lax.axis_size("solve")
    leaf_count = beliefs.shape[0]
    hand_count = regrets.shape[1]
    line_count = regrets.shape[0] * devices
    hidden = jax.nn.silu(
        jnp.dot(
            beliefs,
            lax.all_gather(encoder, "solve", axis=1, tiled=True),
            preferred_element_type=F32,
        )
    ).astype(BF16)
    output = jnp.dot(
        hidden,
        lax.all_gather(value_head, "solve", axis=0, tiled=True),
        preferred_element_type=F32,
    )
    errors = ((output - targets.astype(F32)) / leaf_count).astype(BF16)
    head_grad = lax.psum_scatter(
        lax.dot_general(hidden, errors, (((0,), (0,)), ((), ())), preferred_element_type=F32),
        "solve", scatter_dimension=0, tiled=True,
    )
    card_onehot = (turn_card[:, None] == jnp.arange(52, dtype=jnp.int32)[None, :]).astype(BF16)
    blocked = jnp.dot(
        card_onehot, jnp.asarray(blocker_table(hand_count), dtype=BF16), preferred_element_type=F32
    )
    shown = (1.0 - blocked).astype(BF16)
    weighted = output.astype(BF16) * jnp.concatenate([shown, shown], 1)
    line_onehot = (leaf_line[:, None] == jnp.arange(line_count, dtype=jnp.int32)[None, :]).astype(BF16)
    line_values = lax.psum_scatter(
        lax.dot_general(
            line_onehot, weighted, (((0,), (0,)), ((), ())), preferred_element_type=F32
        ) / open_turns,
        "solve", scatter_dimension=0, tiled=True,
    )
    positive = jnp.maximum(regrets, 0.0) + regret_floor
    denominator, numerator = lax.psum(
        (jnp.sum(positive, 0), jnp.sum(positive * line_values[:, :hand_count], 0)), "solve"
    )
    new_regrets = regrets + line_values[:, :hand_count] - (numerator / denominator)[None, :]
    return (new_regrets, line_values, head_grad)


def solution(mesh):
    split = P(("groups", "solve"), None)
    placed = (
        split, split, P(("groups", "solve")), P(("groups", "solve")),
        P(None, "solve"), P("solve", None), split,
    )
    in_tree = mesh.shape["groups"] == 1 and mesh.shape["solve"] == 32
    return jax.shard_map(
        functools.partial(fused, mesh.shape["solve"] // 8) if in_tree else by_collectives,
        mesh=mesh,
        in_specs=placed,
        out_specs=(split, split, split),
        check_vma=False,
    )
```

time: 444 us -> 127 us (0.29)
  waiting for transfers between devices: 349 us -> 0 us
  Pallas kernels: 0 us -> 113 us
  blocking collectives: 41.3 us -> 0 us
  matrix products: 32.8 us -> 0 us
  between operations: 13.8 us -> 0.64 us
  local copies, waits for them, and re-layouts: 3.85 us -> 13.4 us
    all_gather x2 -> x0, waiting for transfers between devices: 128 us -> none  [the longest x1 67.1 us: per_device(): lax.all_gather(encoder, 'solve', axis=1, tiled=True)]
    unnamed x5 -> x0, waiting for transfers between devices: 114 us -> none
    pallas_call x0 -> x1, Pallas kernels: none -> 113 us  [fused(): pl.pallas_call(functools.partial(step_kernel, nz, hands), out_shape=(jax....]
    reduce_scatter x1 -> x0, waiting for transfers between devices: 107 us -> none  [per_device(): lax.psum_scatter(lax.dot_general(hidden, errors, (((0,), (0,)), ((), ()))...]
    psum x1 -> x0, blocking collectives: 41.3 us -> none  [per_device(): lax.psum((jnp.sum(positive, 0), jnp.sum(positive * line_values[:, :hand_c...]
    dot_general x5 -> x0, matrix products: 32.8 us -> none  [the longest x1 11.7 us: per_device(): lax.dot_general(hidden, errors, (((0,), (0,)), ((), ())), preferred_eleme...]
    unnamed x11 -> x7, local copies, waits for them, and re-layouts: 3.85 us -> 11.9 us
  transfers between devices with their start and end apart: 4 -> 0, of which waited for: 4 -> 0; matrix products, arithmetic and copies ran while one was open for 6% -> 0% of each run, Pallas kernels for 0% -> 0%
where the time goes in v1:
time: 127 us
  Pallas kernels  113 us (89%)
  local copies, waits for them, and re-layouts  13.4 us (11%)
    pallas_call x1, Pallas kernels, fused(): pl.pallas_call(functools.partial(step_kernel, nz, hands), out_shape=(jax....  113 us
    unnamed x7, local copies, waits for them, and re-layouts  11.9 us

profile of v1, /device:TPU:0, one launch (start us, length us, event | category | flops | bytes accessed | tf_op | source)
XLA Modules:
  0.0 127.1 jit_solution(3168253700761528423)
XLA Ops:
  0.6 1.5 %copy.15.card = s32[512,1]{1,0:T(8,128)} copy(s32[512,1]{0,1:T(1,128)} %bitcast.3) | data formatting | bytes 4096 | tf_op jit(solution)/shard_map/reshape | solution.py:365
  2.2 0.0 copy-start
  2.2 4.6 %copy.13.beliefs = bf16[512,2652]{1,0:T(8,128)(2,1)} copy(bf16[512,2652]{0,1:T(8,128)(2,1)} %param.8) | data formatting | bytes 5431296 | tf_op args[0]
  6.8 0.0 copy-done
  6.8 2.9 %copy.14.targets = bf16[512,2652]{1,0:T(8,128)(2,1)} copy(bf16[512,2652]{0,1:T(8,128)(2,1)S(1)} %copy-done) | data formatting | bytes 5431296 | tf_op args[1]
  9.7 113.0 %shard_map.103 = (f32[1,1326]{1,0:T(1,128)}, f32[1,2652]{1,0:T(1,128)}, f32[32,2652]{1,0:T(8,128)}) custom-call(bf16[512,2652]{1,0:T(8,128)(2,1)} %copy.13.beliefs, bf16[512,2652]{1,0:T(8,128)(2,1)} %copy.14.targets, s32[1,512]{1,0:T(1,128)} %bitcast.5, s32[512,1]{1,0:T(8,128)} %copy.15.card, bf16[32,2652]{1,0:T(8,128)(2,1)} %bitcast.4, ...), custom_call_target="tpu_custom_call" | custom-call | flops 8342470656 | bytes 12582912 | tf_op jit(solution)/shard_map/pallas_call | solution.py:322
  122.8 1.3 %copy.19 = f32[1,1326]{1,0:T(1,128)} copy(f32[1,1326]{1,0:T(1,128)} %get-tuple-element.6) | data formatting | bytes 10608
  124.0 1.3 %copy.20 = f32[1,2652]{1,0:T(1,128)} copy(f32[1,2652]{1,0:T(1,128)} %get-tuple-element.7) | data formatting | bytes 21216
  125.3 1.7 %copy.21 = f32[32,2652]{1,0:T(8,128)} copy(f32[32,2652]{1,0:T(8,128)} %get-tuple-element.8) | data formatting | bytes 678912
Async XLA Ops:
  2.2 4.6 %copy-start = (bf16[512,2652]{0,1:T(8,128)(2,1)S(1)}, bf16[512,2652]{0,1:T(8,128)(2,1)}, u32[]{:S(2)}) copy-start(bf16[512,2652]{0,1:T(8,128)(2,1)} %param.9) | copy-start | bytes 8146948

commit v2 on v1

v2 whole, which is shorter than its diff:
```python
import functools

import jax
import jax.numpy as jnp
import numpy as np
from jax import lax
from jax.experimental import pallas as pl
from jax.experimental.pallas import tpu as pltpu
from jax.sharding import PartitionSpec as P

open_turns = 45.0
regret_floor = 0.05
MESH = pl.DeviceIdType.MESH
F32, BF16 = jnp.float32, jnp.bfloat16


def blocker_table(hand_count, rows=52):
    blockers = np.zeros((rows, hand_count), np.float32)
    column = 0
    for low_card in range(52):
        for high_card in range(low_card + 1, 52):
            blockers[low_card, column] = 1.0
            blockers[high_card, column] = 1.0
            column = column + 1
    return blockers


def step_kernel(
    nz, hands,
    beliefs, targets, line, card, enc, head, regrets, blockers,
    new_regrets, line_values, head_grad,
    beliefs_t, targets_t, w1, w2, opened, leaf, errors, hidden, hidden_t, partial,
    sib_send, sib_recv, diag_send, diag_recv, xy_send, xy_recv, z_send, z_recv,
    line_tree, line_in, y_send, y_in, lz_send, lz_in, sums, sums_in,
    ag_s, ag_r, rs_s, rs_r, small_s, small_r, load_s,
):
    n = nz * 8
    rows = enc.shape[0]
    half = rows // 2
    plane = rows * 8
    width, leaves = beliefs.shape
    me = lax.axis_index("solve")
    c = lax.rem(me, 2)
    x = lax.rem(me // 2, 2)
    y = lax.rem(me // 4, 2)
    z = me // 8

    def dev(zz, yy, xx, cc):
        return zz * 8 + yy * 4 + xx * 2 + cc

    z_low, z_high = lax.rem(z, 2), z // 2
    zs = (z, z + 1 - 2 * z_low, z + 2 - 4 * z_high, 3 - z)

    sib, xn, yn = dev(z, y, x, 1 - c), dev(z, y, 1 - x, c), dev(z, 1 - y, x, c)

    zp = tuple(dev(zz, y, x, c) for zz in zs)

    def block(d, start=0, count=rows):
        return pl.ds(pl.multiple_of(d * rows + start, 16), count)

    def remote(src, dst, ss, rs, to):
        return pltpu.make_async_remote_copy(
            src_ref=src, dst_ref=dst, send_sem=ss, recv_sem=rs,
            device_id={"solve": to}, device_id_type=MESH,
        )

    loads = [
        pltpu.make_async_copy(beliefs, beliefs_t, load_s.at[0]),
        pltpu.make_async_copy(targets, targets_t, load_s.at[1]),
    ]
    for load in loads:
        load.start()

    barrier = pltpu.get_barrier_semaphore()
    for to in (*zp[1:], xn, yn, sib):
        pl.semaphore_signal(barrier, inc=1, device_id={"solve": to}, device_id_type=MESH)
    pl.semaphore_wait(barrier, 6)

    started = []
    used = [0, 0]

    def gather_send(k, src_dev, to, part=None, own=None):
        w = (w1, w2)[k]
        span = (0, rows) if part is None else (part * half, half)
        place = w.at[block(src_dev, *span)]
        slot = used[k]
        used[k] += 1
        rsem = ag_r.at[k, src_dev] if part != 1 else ag_r.at[k, n + src_dev // 8]
        cp = remote(place if own is None else own, place, ag_s.at[k, slot], rsem, to)
        cp.start()
        started.append(cp)

    def gather_wait(k, src_dev, part=None):
        w = (w1, w2)[k]
        span = (0, rows) if part is None else (part * half, half)
        place = w.at[block(src_dev, *span)]
        rsem = ag_r.at[k, src_dev] if part != 1 else ag_r.at[k, n + src_dev // 8]
        remote(place, place, ag_s.at[k, 0], rsem, sib).wait_recv()

    for k, own in ((0, enc), (1, head)):
        for to in (zp[1], xn, yn, zp[2], zp[3], sib):
            gather_send(k, me, to, own=own)
    w1[block(me)] = enc[...]
    w2[block(me)] = head[...]

    def forward_column(k, q):
        src = dev(zs[q], y, x, c)
        gather_wait(k, src)
        for to in (sib,) if q == 1 else (xn, yn, sib):
            gather_send(k, src, to)

    def forward_plane(k, q):
        src = dev(zs[q], y, 1 - x, c)
        gather_wait(k, src)
        if q == 0:
            gather_send(k, src, zp[1])
        gather_send(k, src, yn, part=0)
        gather_send(k, src, sib)
        src = dev(zs[q], 1 - y, x, c)
        gather_wait(k, src)
        if q == 0:
            gather_send(k, src, zp[1])
        gather_send(k, src, xn, part=1)
        gather_send(k, src, sib)

    def forward_diagonal(k, q):
        src = dev(zs[q], 1 - y, 1 - x, c)
        gather_wait(k, src, 0)
        gather_wait(k, src, 1)
        gather_send(k, src, sib)

    def wait_sibling(k, dz):
        for yy in (0, 1):
            for xx in (0, 1):
                gather_wait(k, dev(zs[dz], yy, xx, 1 - c))

    forward_plane(0, 0)
    for q in (1, 2, 3):
        forward_column(0, q)
    forward_plane(1, 0)
    for q in (1, 2, 3):
        forward_column(1, q)
    for q in (1, 2, 3):
        forward_plane(0, q)
    for q in (1, 2, 3):
        forward_plane(1, q)

    card_onehot = (
        lax.broadcasted_iota(jnp.int32, (blockers.shape[0], leaves), 0) == card[...]
    ).astype(F32).T.astype(BF16)
    for start in range(0, width, 256):
        cols = slice(start, min(start + 256, width))
        opened[:, cols] = (
            1.0 - jnp.dot(card_onehot, blockers[:, cols], preferred_element_type=F32)
        ).astype(BF16)
    for q in range(4):
        forward_diagonal(0, q)

    for load in loads:
        load.wait()
    for q in range(4):
        wait_sibling(0, q)
        units = pl.ds(pl.multiple_of(zs[q] * plane, plane), plane)
        pre = jnp.dot(w1[units, :], beliefs_t[...], preferred_element_type=F32)
        act = pre / (1.0 + jnp.exp(-pre))
        hidden_t[units, :] = act.astype(BF16)
        hidden[:, units] = act.T.astype(BF16)
        forward_diagonal(1, q)
    for start in range(0, width, 256):
        cols = slice(start, min(start + 256, width))
        errors[:, cols] = targets_t[cols, :].astype(F32).T.astype(BF16)
    for q in range(4):
        wait_sibling(1, q)

    def output_columns(cols):
        out = jnp.dot(hidden[...], w2[:, cols], preferred_element_type=F32)
        errors[:, cols] = ((out - errors[:, cols].astype(F32)) * (1.0 / leaves)).astype(BF16)
        leaf[:, cols] = out.astype(BF16)

    full = width // 256

    def output_step(j, _):
        output_columns(pl.ds(pl.multiple_of(j * 256, 256), 256))
        return _

    lax.fori_loop(0, full, output_step, 0)
    if full * 256 < width:
        output_columns(slice(full * 256, width))

    order = (1, 2, 3, 0)
    pend = {}
    rs_used = [0]

    def reduce_send(name, src, dst, to):
        slot = rs_used[0]
        rs_used[0] += 1
        cp = remote(src, dst, rs_s.at[slot], rs_r.at[slot], to)
        cp.start()
        started.append(cp)
        pend[name] = cp

    def in_plane(yy, xx, cc):
        return pl.ds(pl.multiple_of((yy * 4 + xx * 2 + cc) * rows, rows), rows)

    rel = ((y, x), (y, 1 - x), (1 - y, x), (1 - y, 1 - x))

    def compute(p):
        units = pl.ds(pl.multiple_of(zs[order[p]] * plane, plane), plane)
        partial[p] = jnp.dot(hidden_t[units, :], errors[...], preferred_element_type=F32)
        for r in (3, 1, 2, 0):
            yy, xx = rel[r]
            sib_send[p, r] = partial[p, in_plane(yy, xx, 1 - c)].astype(BF16)
            reduce_send(("s", p, r), sib_send.at[p, r], sib_recv.at[p, r], sib)

    def chip_sum(p, r, lo=0, count=rows):
        yy, xx = rel[r]
        base = (yy * 4 + xx * 2 + c) * rows + lo
        own = partial[p, pl.ds(pl.multiple_of(base, 16), count)]
        return own + sib_recv[p, r, lo:lo + count].astype(F32)

    def stage_diagonal(p):
        pend["s", p, 3].wait_recv()
        diag_send[p] = chip_sum(p, 3).astype(BF16)
        reduce_send(("a", p), diag_send.at[p, pl.ds(0, half)], diag_recv.at[p, pl.ds(0, half)], yn)
        reduce_send(("b", p), diag_send.at[p, pl.ds(half, half)], diag_recv.at[p, pl.ds(half, half)], xn)

    def stage_neighbours(p):
        for r, name, to, lo in ((1, "a", xn, 0), (2, "b", yn, half)):
            pend["s", p, r].wait_recv()
            pend[name, p].wait_recv()
            total = chip_sum(p, r)
            there = diag_recv[p, lo:lo + half].astype(F32)
            keep = total[half - lo:half - lo + half]
            mixed = total[lo:lo + half] + there
            if p == 3:
                pend["n", 0, r].wait_recv()
                extra = xy_recv[0, r - 1].astype(F32)
                mixed += extra[lo:lo + half]
                keep += extra[half - lo:half - lo + half]
            xy_send[p, r - 1, lo:lo + half] = mixed.astype(BF16)
            xy_send[p, r - 1, half - lo:half - lo + half] = keep.astype(BF16)
            reduce_send(("n", p, r), xy_send.at[p, r - 1], xy_recv.at[p, r - 1], zp[1] if p == 0 else to)

    def column_sum(p):
        pend["s", p, 0].wait_recv()
        total = chip_sum(p, 0)
        if p > 0:
            for r in (1, 2):
                pend["n", p, r].wait_recv()
                total += xy_recv[p, r - 1].astype(F32)
        return total

    def stage_column(p):
        z_send[p] = column_sum(p).astype(BF16)
        reduce_send(("z", p), z_send.at[p], z_recv.at[p], zp[order[p]])

    small = {}
    small_used = [0]

    def small_send(name, src, dst, to):
        slot = small_used[0]
        small_used[0] += 1
        cp = remote(src, dst, small_s.at[slot], small_r.at[slot], to)
        cp.start()
        started.append(cp)
        small[name] = cp

    def flip(bit, by):
        return bit + by - 2 * bit * by

    def line_terms():
        r = lax.broadcasted_iota(jnp.int32, (n, leaves), 0)
        far = [lax.rem(r // 2 ** b, 2) for b in range(5)]
        owner = (
            16 * flip(z_high, far[1]) + 8 * flip(z_low, far[0])
            + 4 * flip(y, far[2]) + 2 * flip(x, far[3]) + flip(c, far[4])
        )
        onehot = (owner == line[...]).astype(F32).astype(BF16)
        for start in range(0, width, 512):
            cols = slice(start, min(start + 512, width))
            masked = (leaf[:, cols].astype(F32) * opened[:, cols].astype(F32)).astype(BF16)
            line_tree[:, cols] = jnp.dot(onehot, masked, preferred_element_type=F32) / open_turns
        small_send("lc", line_tree.at[pl.ds(16, 16)], line_in.at[pl.ds(16, 16)], sib)

    def line_x():
        small["lc"].wait_recv()
        line_tree[0:16] += line_in[16:32]
        small_send("lx", line_tree.at[pl.ds(8, 8)], line_in.at[pl.ds(8, 8)], xn)

    def line_y():
        small["lx"].wait_recv()
        both = line_tree[0:8] + line_in[8:16]
        line_tree[0:8] = both
        y_send[0:4] = both[4:8]
        small_send("ly", y_send, y_in, yn)

    def line_z():
        small["ly"].wait_recv()
        four = line_tree[0:4] + y_in[0:4]
        line_tree[0:4] = four
        for q in (1, 2, 3):
            lz_send[q - 1] = four[q:q + 1]
            small_send(("lz", q), lz_send.at[q - 1], lz_in.at[q - 1], zp[q])

    positive = jnp.maximum(regrets[...], 0.0) + regret_floor

    def line_done():
        value = line_tree[0:1]
        for q in (1, 2, 3):
            small["lz", q].wait_recv()
            value += lz_in[q - 1]
        line_values[...] = value
        sums[0, 0:1] = positive * value[:, :hands]
        sums[0, 1:2] = positive
        small_send("nc", sums.at[0], sums_in.at[0], sib)

    def sums_step(at, name, following, to):
        small[name].wait_recv()
        sums[at, 0:2] = sums[at - 1, 0:2] + sums_in[at - 1, 0:2]
        for q, dst in enumerate(to):
            small_send((following, q), sums.at[at], sums_in.at[at + q], dst)

    def root_done():
        total = sums[3, 0:2]
        for q in (0, 1, 2):
            small["nz", q].wait_recv()
            total += sums_in[3 + q, 0:2]
        root = total[0:1] / total[1:2]
        new_regrets[...] = regrets[...] + line_values[:, :hands] - root

    y_send[4:8] = jnp.zeros((4, width), F32)
    sums[...] = jnp.zeros_like(sums)
    compute(0)
    compute(1)
    stage_diagonal(0)
    compute(2)
    stage_diagonal(1)
    stage_neighbours(0)
    compute(3)
    stage_diagonal(2)
    stage_neighbours(1)
    stage_column(0)
    stage_diagonal(3)
    line_terms()
    stage_neighbours(2)
    line_x()
    stage_column(1)
    line_y()
    stage_neighbours(3)
    line_z()
    stage_column(2)
    line_done()
    sums_step(1, "nc", "nx", (xn,))
    sums_step(2, ("nx", 0), "ny", (yn,))
    sums_step(3, ("ny", 0), "nz", zp[1:])
    root_done()

    result = column_sum(3)
    for p in range(3):
        pend["z", p].wait_recv()
        result += z_recv[p].astype(F32)
    head_grad[...] = result

    for cp in started:
        cp.wait_send()

def fused(nz, beliefs, targets, leaf_line, turn_card, encoder, value_head, regrets):
    n = nz * 8
    leaves, width = beliefs.shape
    hands = regrets.shape[1]
    rows = value_head.shape[0]
    units = rows * n
    table = blocker_table(hands, 64)
    blockers = jnp.asarray(np.concatenate([table, table], 1), dtype=BF16)
    vm = pl.BlockSpec(memory_space=pltpu.VMEM)
    dma = pltpu.SemaphoreType.DMA
    outs = pl.pallas_call(
        functools.partial(step_kernel, nz, hands),
        out_shape=(
            jax.ShapeDtypeStruct((1, hands), F32),
            jax.ShapeDtypeStruct((1, width), F32),
            jax.ShapeDtypeStruct((rows, width), F32),
        ),
        in_specs=[pl.BlockSpec(memory_space=pl.ANY)] * 2 + [vm] * 6,
        out_specs=(vm, vm, vm),
        scratch_shapes=[
            pltpu.VMEM((width, leaves), BF16),
            pltpu.VMEM((width, leaves), BF16),
            pltpu.VMEM((units, width), BF16),
            pltpu.VMEM((units, width), BF16),
            pltpu.VMEM((leaves, width), BF16),
            pltpu.VMEM((leaves, width), BF16),
            pltpu.VMEM((leaves, width), BF16),
            pltpu.VMEM((leaves, units), BF16),
            pltpu.VMEM((units, leaves), BF16),
            pltpu.VMEM((4, rows * 8, width), F32),
            pltpu.VMEM((4, 4, rows, width), BF16),
            pltpu.VMEM((4, 4, rows, width), BF16),
            pltpu.VMEM((4, rows, width), BF16),
            pltpu.VMEM((4, rows, width), BF16),
            pltpu.VMEM((4, 2, rows, width), BF16),
            pltpu.VMEM((4, 2, rows, width), BF16),
            pltpu.VMEM((3, rows, width), BF16),
            pltpu.VMEM((3, rows, width), BF16),
            pltpu.VMEM((n, width), F32),
            pltpu.VMEM((n, width), F32),
            pltpu.VMEM((8, width), F32),
            pltpu.VMEM((8, width), F32),
            pltpu.VMEM((3, 1, width), F32),
            pltpu.VMEM((3, 1, width), F32),
            pltpu.VMEM((4, 8, hands), F32),
            pltpu.VMEM((6, 8, hands), F32),
            dma((2, 40)),
            dma((2, n + nz)),
            dma((40,)),
            dma((40,)),
            dma((16,)),
            dma((16,)),
            dma((2,)),
        ],
        compiler_params=pltpu.CompilerParams(
            collective_id=0, has_side_effects=True, vmem_limit_bytes=62 * 2**20
        ),
        cost_estimate=pl.CostEstimate(
            flops=6 * leaves * width * units, bytes_accessed=12 * 2**20, transcendentals=leaves * units
        ),
    )(
        beliefs.T, targets.T, leaf_line.reshape(1, leaves), turn_card.reshape(1, leaves),
        encoder.T, value_head, regrets, blockers,
    )
    return pl.pallas_call(
        hand_over, out_shape=tuple(jax.ShapeDtypeStruct(o.shape, o.dtype) for o in outs), in_specs=[vm] * 3, out_specs=(vm, vm, vm)
    )(*outs)


def hand_over(a, b, c, a_out, b_out, c_out):
    a_out[...] = a[...]
    b_out[...] = b[...]
    c_out[...] = c[...]


def by_collectives(beliefs, targets, leaf_line, turn_card, encoder, value_head, regrets):
    devices = lax.axis_size("solve")
    leaf_count = beliefs.shape[0]
    hand_count = regrets.shape[1]
    line_count = regrets.shape[0] * devices
    hidden = jax.nn.silu(
        jnp.dot(
            beliefs,
            lax.all_gather(encoder, "solve", axis=1, tiled=True),
            preferred_element_type=F32,
        )
    ).astype(BF16)
    output = jnp.dot(
        hidden,
        lax.all_gather(value_head, "solve", axis=0, tiled=True),
        preferred_element_type=F32,
    )
    errors = ((output - targets.astype(F32)) / leaf_count).astype(BF16)
    head_grad = lax.psum_scatter(
        lax.dot_general(hidden, errors, (((0,), (0,)), ((), ())), preferred_element_type=F32),
        "solve", scatter_dimension=0, tiled=True,
    )
    card_onehot = (turn_card[:, None] == jnp.arange(52, dtype=jnp.int32)[None, :]).astype(BF16)
    blocked = jnp.dot(
        card_onehot, jnp.asarray(blocker_table(hand_count), dtype=BF16), preferred_element_type=F32
    )
    shown = (1.0 - blocked).astype(BF16)
    weighted = output.astype(BF16) * jnp.concatenate([shown, shown], 1)
    line_onehot = (leaf_line[:, None] == jnp.arange(line_count, dtype=jnp.int32)[None, :]).astype(BF16)
    line_values = lax.psum_scatter(
        lax.dot_general(
            line_onehot, weighted, (((0,), (0,)), ((), ())), preferred_element_type=F32
        ) / open_turns,
        "solve", scatter_dimension=0, tiled=True,
    )
    positive = jnp.maximum(regrets, 0.0) + regret_floor
    denominator, numerator = lax.psum(
        (jnp.sum(positive, 0), jnp.sum(positive * line_values[:, :hand_count], 0)), "solve"
    )
    new_regrets = regrets + line_values[:, :hand_count] - (numerator / denominator)[None, :]
    return (new_regrets, line_values, head_grad)


def solution(mesh):
    split = P(("groups", "solve"), None)
    placed = (
        split, split, P(("groups", "solve")), P(("groups", "solve")),
        P(None, "solve"), P("solve", None), split,
    )
    in_tree = mesh.shape["groups"] == 1 and mesh.shape["solve"] == 32
    return jax.shard_map(
        functools.partial(fused, mesh.shape["solve"] // 8) if in_tree else by_collectives,
        mesh=mesh,
        in_specs=placed,
        out_specs=(split, split, split),
        check_vma=False,
    )
```

time: 127 us -> 108 us (0.85)
  local copies, waits for them, and re-layouts: 13.4 us -> 0 us
  Pallas kernels: 113 us -> 107 us
    unnamed x7 -> x0, local copies, waits for them, and re-layouts: 11.9 us -> none
    pallas_call x1, Pallas kernels: 113 us -> 106 us  [fused(): pl.pallas_call(functools.partial(step_kernel, nz, hands), out_shape=(jax....]
    pallas_call x0 -> x1, Pallas kernels: none -> 1.77 us  [fused(): pl.pallas_call(hand_over, out_shape=tuple((jax.ShapeDtypeStruct(o.shape,...]
    reshape x1 -> x0, local copies, waits for them, and re-layouts: 1.54 us -> none  [fused(): turn_card.reshape(leaves, 1)]
where the time goes in v2:
time: 108 us
  Pallas kernels  107 us (99%)
    pallas_call x1, Pallas kernels, fused(): pl.pallas_call(functools.partial(step_kernel, nz, hands), out_shape=(jax....  106 us

profile of v2, /device:TPU:0, one launch (start us, length us, event | category | flops | bytes accessed | tf_op | source)
XLA Modules:
  0.0 108.0 jit_solution(7617746705866875041)
XLA Ops:
  0.6 105.6 %shard_map.103 = (f32[1,1326]{1,0:T(1,128)}, f32[1,2652]{1,0:T(1,128)}, f32[32,2652]{1,0:T(8,128)}) custom-call(bf16[2652,512]{1,0:T(8,128)(2,1)} %bitcast.5, bf16[2652,512]{1,0:T(8,128)(2,1)} %bitcast.6, s32[1,512]{1,0:T(1,128)} %bitcast.8, s32[1,512]{1,0:T(1,128)} %bitcast.9, bf16[32,2652]{1,0:T(8,128)(2,1)} %bitcast.7, bf16[32,2652]{1,0:T(8,128)(2,1)} %head.1, ...), custom_call_target="tpu_custom_call" | custom-call | flops 8342470656 | bytes 12582912 | tf_op jit(solution)/shard_map/pallas_call | solution.py:377
  106.2 1.8 %shard_map.104 = (f32[1,1326]{1,0:T(1,128)}, f32[1,2652]{1,0:T(1,128)}, f32[32,2652]{1,0:T(8,128)}) custom-call(f32[1,1326]{1,0:T(1,128)} %get-tuple-element.6.a, f32[1,2652]{1,0:T(1,128)} %get-tuple-element.7.b, f32[32,2652]{1,0:T(8,128)} %get-tuple-element.8.c), custom_call_target="tpu_custom_call" | custom-call | tf_op jit(solution)/shard_map/pallas_call | solution.py:431

commit v3 on v2

--- a/solution.py
+++ b/solution.py
@@ -332,26 +332,26 @@
     sums[...] = jnp.zeros_like(sums)
     compute(0)
     compute(1)
+    line_terms()
     stage_diagonal(0)
     compute(2)
+    line_x()
     stage_diagonal(1)
     stage_neighbours(0)
+    line_y()
     compute(3)
     stage_diagonal(2)
     stage_neighbours(1)
+    line_z()
     stage_column(0)
     stage_diagonal(3)
-    line_terms()
+    line_done()
     stage_neighbours(2)
-    line_x()
+    sums_step(1, "nc", "nx", (xn,))
     stage_column(1)
-    line_y()
     stage_neighbours(3)
-    line_z()
+    sums_step(2, ("nx", 0), "ny", (yn,))
     stage_column(2)
-    line_done()
-    sums_step(1, "nc", "nx", (xn,))
-    sums_step(2, ("nx", 0), "ny", (yn,))
     sums_step(3, ("ny", 0), "nz", zp[1:])
     root_done()
 

time: 108 us -> 105 us (0.972)
  Pallas kernels: 107 us -> 104 us
    pallas_call x1, Pallas kernels: 106 us -> 103 us  [fused(): pl.pallas_call(functools.partial(step_kernel, nz, hands), out_shape=(jax....]
where the time goes in v3:
time: 105 us
  Pallas kernels  104 us (99%)
    pallas_call x1, Pallas kernels, fused(): pl.pallas_call(functools.partial(step_kernel, nz, hands), out_shape=(jax....  103 us

profile of v3, /device:TPU:0, one launch (start us, length us, event | category | flops | bytes accessed | tf_op | source)
XLA Modules:
  0.0 104.9 jit_solution(1840601215022869032)
XLA Ops:
  0.6 102.5 %shard_map.103 = (f32[1,1326]{1,0:T(1,128)}, f32[1,2652]{1,0:T(1,128)}, f32[32,2652]{1,0:T(8,128)}) custom-call(bf16[2652,512]{1,0:T(8,128)(2,1)} %bitcast.5, bf16[2652,512]{1,0:T(8,128)(2,1)} %bitcast.6, s32[1,512]{1,0:T(1,128)} %bitcast.8, s32[1,512]{1,0:T(1,128)} %bitcast.9, bf16[32,2652]{1,0:T(8,128)(2,1)} %bitcast.7, bf16[32,2652]{1,0:T(8,128)(2,1)} %head.1, ...), custom_call_target="tpu_custom_call" | custom-call | flops 8342470656 | bytes 12582912 | tf_op jit(solution)/shard_map/pallas_call | solution.py:377
  103.2 1.8 %shard_map.104 = (f32[1,1326]{1,0:T(1,128)}, f32[1,2652]{1,0:T(1,128)}, f32[32,2652]{1,0:T(8,128)}) custom-call(f32[1,1326]{1,0:T(1,128)} %get-tuple-element.6.a, f32[1,2652]{1,0:T(1,128)} %get-tuple-element.7.b, f32[32,2652]{1,0:T(8,128)} %get-tuple-element.8.c), custom_call_target="tpu_custom_call" | custom-call | tf_op jit(solution)/shard_map/pallas_call | solution.py:431
